TPU v7x, 128 devices: a whole 4x4x4 slice. The times are simulated.
128 devices in a mesh: dp: 16 (over z_hi, y, core), fsdp: 8 (over z_lo, x).
Axes of the slice: x: 4, y: 4, z: 4 (z_hi: 2, z_lo: 2; z = z_hi * 2 + z_lo), core: 2. Of those that a mesh axis runs over, the one named last changes fastest.
Arguments:
- block_in: bfloat16 [2, 16, 1024, 1024], P(None, 'dp', 'fsdp'), may hold values from -6 to 6
- cotangent: float32 [2, 16, 1024, 1024], P(None, 'dp', 'fsdp'), may hold values from -6 to 6
- lengths: int32 [2, 16], P(None, 'dp'), may hold values from 512 to 1024, as said below
- vector_params: float32 [5, 1024], replicated
- vector_first: float32 [5, 1024], replicated, may hold values from -448 to 448
- vector_second: float32 [5, 1024], replicated, may hold values from 6144 to 24576
- w_in: bfloat16 [1024, 3072], P('fsdp'), may hold values from -0.1875 to 0.1875
- w_out: bfloat16 [1024, 1024], P('fsdp'), may hold values from -0.1875 to 0.1875
- w_gate: bfloat16 [1024, 4608], P('fsdp'), may hold values from -0.1875 to 0.1875
- w_up: bfloat16 [1024, 4608], P('fsdp'), may hold values from -0.1875 to 0.1875
- w_down: bfloat16 [1024, 4608], P('fsdp'), may hold values from -0.09375 to 0.09375
- tile_owner: int32 [8, 140], P('fsdp'), may hold values from 0 to 15, as said below
- tile_master: float32 [8, 192, 128, 128], P('fsdp', 'dp'), may hold values from -0.4375 to 0.4375
- tile_first: float32 [8, 192, 128, 128], P('fsdp', 'dp'), may hold values from -448 to 448
- tile_second: float32 [8, 192, 128, 128], P('fsdp', 'dp'), may hold values from 6144 to 24576
- tile_stats: float32 [8, 192, 2, 128, 128], P('fsdp', 'dp'), as said below
- tile_bases: float32 [8, 192, 2, 128, 128], P('fsdp', 'dp'), as said below
Outputs:
- block_out: float32 [2, 16, 1024, 1024], P(None, 'dp', 'fsdp')
- grad_in: float32 [2, 16, 1024, 1024], P(None, 'dp', 'fsdp')
- vector_new: float32 [5, 1024], replicated
- vector_first_new: float32 [5, 1024], replicated
- vector_second_new: float32 [5, 1024], replicated
- w_in_new: bfloat16 [1024, 3072], P('fsdp')
- w_out_new: bfloat16 [1024, 1024], P('fsdp')
- w_gate_new: bfloat16 [1024, 4608], P('fsdp')
- w_up_new: bfloat16 [1024, 4608], P('fsdp')
- w_down_new: bfloat16 [1024, 4608], P('fsdp')
- tile_master_new: float32 [8, 192, 128, 128], P('fsdp', 'dp')
- tile_first_new: float32 [8, 192, 128, 128], P('fsdp', 'dp')
- tile_second_new: float32 [8, 192, 128, 128], P('fsdp', 'dp')
- tile_stats_new: float32 [8, 192, 2, 128, 128], P('fsdp', 'dp')
- tile_bases_new: float32 [8, 192, 2, 128, 128], P('fsdp', 'dp')
Inputs may be any that keep to these rules, and one draw needn't show every extreme that they name: `lengths`: positions below a sequence's length are live, the rest padding; in each sequence index some micro-batch is full, and some entry is 512. `tile_owner`: no owner gets more than 12 tiles of one shard; in every shard one owner gets exactly 12. `tile_stats`: each matrix is symmetric positive definite. `tile_bases`: each matrix is orthogonal.
All inputs are finite; a program needn't handle non-finite values.
Results may differ from a plain program's by a relative error of at most 0.0085.
Values may be sent and summed in bfloat16 or wider, within the bound.
No kernel may reach another device: no remote copies, remote signals or barrier semaphores. Data moves between devices by JAX's collectives and lax.ppermute only.
A program may use at most 768 MiB of HBM per device.

v0:
```python
from functools import reduce

import jax
import jax.numpy as jnp
from jax import lax
from jax.sharding import PartitionSpec as P

STEP = 10


EPS_NORM = 1e-05
EPS_ADAM = 1e-08
BETA_ONE = 0.5
BETA_TWO = 0.5
BETA_STAT = 0.5
RATE_MATRIX = 0.03
RATE_VECTOR = 0.2
DECAY_WEIGHT = 0.01
PRECISE = lax.Precision.HIGHEST
BACK_DIMS = (((1,), (1,)), ((), ()))
TOKEN_DIMS = (((0,), (0,)), ((), ()))


def from_behind(value, axis, by):
    length = lax.axis_size(axis)
    pairs = [(i, i + by) for i in range(length) if 0 <= i + by < length]
    return lax.ppermute(value, axis, pairs)


def rms_factor(values):
    return lax.rsqrt(jnp.mean(values * values, axis=-1, keepdims=True) + EPS_NORM)


def norm_back(values, scale_val, gain_row, grad_out):
    weighted = grad_out * gain_row
    inner = jnp.mean(values * weighted, axis=-1, keepdims=True)
    grad_values = scale_val * weighted - values * scale_val * scale_val * scale_val * inner
    grad_gain = jnp.sum(values * scale_val * grad_out, axis=0)
    return (grad_values, grad_gain)


def forward_pass(token_rows, vectors, weights):
    w_in, w_out, w_gate, w_up, w_down = weights
    model_width = token_rows.shape[1]
    scale_one = rms_factor(token_rows)
    normed = (token_rows * scale_one * vectors[0]).astype(jnp.bfloat16)
    mixed_all = jnp.dot(normed, w_in, preferred_element_type=jnp.float32)
    part_b = mixed_all[:, :model_width]
    part_c = mixed_all[:, model_width : 2 * model_width]
    part_x = mixed_all[:, 2 * model_width :]
    product = part_b * part_x
    prior_rows = from_behind(product[-2:], "fsdp", 1)
    extended = jnp.concatenate([prior_rows, product], axis=0)
    convolved = vectors[2] * extended[:-2] + vectors[3] * extended[1:-1] + vectors[4] * extended[2:]
    gated_conv = (part_c * convolved).astype(jnp.bfloat16)
    branch = jnp.dot(gated_conv, w_out, preferred_element_type=jnp.float32)
    residual = token_rows + branch
    scale_two = rms_factor(residual)
    normed_two = (residual * scale_two * vectors[1]).astype(jnp.bfloat16)
    gate_val = jnp.dot(normed_two, w_gate, preferred_element_type=jnp.float32)
    up_val = jnp.dot(normed_two, w_up, preferred_element_type=jnp.float32)
    activation = (jax.nn.silu(gate_val) * up_val).astype(jnp.bfloat16)
    ffn_out = lax.dot_general(activation, w_down, BACK_DIMS, preferred_element_type=jnp.float32)
    kept_values = (
        token_rows,
        scale_one,
        normed,
        part_b,
        part_c,
        part_x,
        extended,
        convolved,
        gated_conv,
        residual,
        scale_two,
        normed_two,
        gate_val,
        up_val,
        activation,
    )
    return (residual + ffn_out, kept_values)


def backward_pass(seed_grad, vectors, weights, kept_values):
    w_in, w_out, w_gate, w_up, w_down = weights
    (
        token_rows,
        scale_one,
        normed,
        part_b,
        part_c,
        part_x,
        extended,
        convolved,
        gated_conv,
        residual,
        scale_two,
        normed_two,
        gate_val,
        up_val,
        activation,
    ) = kept_values
    tok_count = seed_grad.shape[0]
    grad_feed = seed_grad.astype(jnp.bfloat16)
    grad_act = jnp.dot(grad_feed, w_down, preferred_element_type=jnp.float32)
    sigmoid_gate = jax.nn.sigmoid(gate_val)
    grad_gate = (grad_act * up_val * sigmoid_gate * (1.0 + gate_val * (1.0 - sigmoid_gate))).astype(
        jnp.bfloat16
    )
    grad_up = (grad_act * gate_val * sigmoid_gate).astype(jnp.bfloat16)
    grad_normed_two = lax.dot_general(
        grad_gate, w_gate, BACK_DIMS, preferred_element_type=jnp.float32
    ) + lax.dot_general(grad_up, w_up, BACK_DIMS, preferred_element_type=jnp.float32)
    grad_res_norm, grad_gain_two = norm_back(residual, scale_two, vectors[1], grad_normed_two)
    grad_resid = seed_grad + grad_res_norm
    grad_branch = grad_resid.astype(jnp.bfloat16)
    grad_gated = lax.dot_general(grad_branch, w_out, BACK_DIMS, preferred_element_type=jnp.float32)
    grad_part_c = grad_gated * convolved
    grad_conv = grad_gated * part_c
    later_rows = from_behind(grad_conv[:2], "fsdp", -1)
    grad_ext = jnp.concatenate([grad_conv, later_rows], axis=0)
    grad_product = (
        vectors[4] * grad_conv
        + vectors[3] * grad_ext[1 : tok_count + 1]
        + vectors[2] * grad_ext[2:]
    )
    grad_kernel = jnp.stack(
        [
            jnp.sum(grad_conv * extended[:-2], axis=0),
            jnp.sum(grad_conv * extended[1:-1], axis=0),
            jnp.sum(grad_conv * extended[2:], axis=0),
        ]
    )
    grad_mixed = jnp.concatenate(
        [grad_product * part_x, grad_part_c, grad_product * part_b], axis=1
    ).astype(jnp.bfloat16)
    grad_normed = lax.dot_general(grad_mixed, w_in, BACK_DIMS, preferred_element_type=jnp.float32)
    grad_rows_norm, grad_gain_one = norm_back(token_rows, scale_one, vectors[0], grad_normed)
    grad_rows = grad_resid + grad_rows_norm
    vector_part = jnp.concatenate([grad_gain_one[None], grad_gain_two[None], grad_kernel], axis=0)
    operands = (
        normed,
        grad_mixed,
        gated_conv,
        grad_branch,
        normed_two,
        grad_gate,
        grad_up,
        grad_feed,
        activation,
    )
    return (grad_rows, vector_part, operands)


def weight_terms(operands):
    (
        normed,
        grad_mixed,
        gated_conv,
        grad_branch,
        normed_two,
        grad_gate,
        grad_up,
        grad_feed,
        activation,
    ) = operands

    def outer_sum(left_arr, right_arr):
        return lax.dot_general(left_arr, right_arr, TOKEN_DIMS, preferred_element_type=jnp.float32)

    return jnp.concatenate(
        [
            outer_sum(normed, grad_mixed),
            outer_sum(gated_conv, grad_branch),
            outer_sum(normed_two, grad_gate),
            outer_sum(normed_two, grad_up),
            outer_sum(grad_feed, activation),
        ],
        axis=1,
    )


def slot_table(owner_row, per_owner):
    tile_count = owner_row.shape[0]
    same_owner = owner_row[None, :] == owner_row[:, None]
    before = (
        jnp.arange(tile_count, dtype=jnp.int32)[None, :]
        < jnp.arange(tile_count, dtype=jnp.int32)[:, None]
    )
    slot_rank = jnp.sum((same_owner & before).astype(jnp.int32), axis=1)
    return owner_row * per_owner + slot_rank


def rotate_into(left_basis, matrix, right_basis):
    step_one = jnp.einsum("sji,sjk->sik", left_basis, matrix, precision=PRECISE)
    return jnp.einsum("sik,skl->sil", step_one, right_basis, precision=PRECISE)


def rotate_back(left_basis, matrix, right_basis):
    step_one = jnp.einsum("sij,sjk->sik", left_basis, matrix, precision=PRECISE)
    return jnp.einsum("sik,slk->sil", step_one, right_basis, precision=PRECISE)


def solve_lower(lower_factor, rhs_matrix):
    return jax.scipy.linalg.solve_triangular(lower_factor, rhs_matrix, lower=True)


def orthonormal(matrix):
    gram = jnp.einsum("sji,sjk->sik", matrix, matrix, precision=PRECISE)
    lower_factor = jnp.linalg.cholesky(gram)
    solved = jax.vmap(solve_lower)(lower_factor, jnp.swapaxes(matrix, 1, 2))
    return jnp.swapaxes(solved, 1, 2)


def soap_update(grad_tiles, master, first, second, stats, bases):
    left_basis = bases[:, 0]
    right_basis = bases[:, 1]
    rotated = rotate_into(left_basis, grad_tiles, right_basis)
    first_new = BETA_ONE * first + (1.0 - BETA_ONE) * grad_tiles
    second_new = BETA_TWO * second + (1.0 - BETA_TWO) * rotated * rotated
    moment_rot = rotate_into(left_basis, first_new, right_basis)
    direction = (
        moment_rot
        / (1.0 - BETA_ONE**STEP)
        / (jnp.sqrt(second_new / (1.0 - BETA_TWO**STEP)) + EPS_ADAM)
    )
    master_new = master - RATE_MATRIX * (
        rotate_back(left_basis, direction, right_basis) + DECAY_WEIGHT * master
    )
    stat_left = BETA_STAT * stats[:, 0] + (1.0 - BETA_STAT) * jnp.einsum(
        "sik,sjk->sij", grad_tiles, grad_tiles, precision=PRECISE
    )
    stat_right = BETA_STAT * stats[:, 1] + (1.0 - BETA_STAT) * jnp.einsum(
        "ski,skj->sij", grad_tiles, grad_tiles, precision=PRECISE
    )
    left_new = orthonormal(jnp.einsum("sij,sjk->sik", stat_left, left_basis, precision=PRECISE))
    right_new = orthonormal(jnp.einsum("sij,sjk->sik", stat_right, right_basis, precision=PRECISE))
    return (
        master_new,
        first_new,
        second_new,
        jnp.stack([stat_left, stat_right], axis=1),
        jnp.stack([left_new, right_new], axis=1),
    )


def shards(
    block_in,
    cotangent,
    lengths,
    vector_params,
    vector_first,
    vector_second,
    w_in,
    w_out,
    w_gate,
    w_up,
    w_down,
    tile_owner,
    tile_master,
    tile_first,
    tile_second,
    tile_stats,
    tile_bases,
):
    micro_count = block_in.shape[0]
    tok_count = block_in.shape[2]
    model_width = block_in.shape[3]
    hidden_width = w_gate.shape[1]
    shard_rows = w_in.shape[0]
    shard_weights = (w_in, w_out, w_gate, w_up, w_down)
    positions = lax.axis_index("fsdp") * tok_count + jnp.arange(tok_count, dtype=jnp.int32)
    outputs = []
    grads_in = []
    vector_terms = []
    batch_terms = []
    for micro_step in range(micro_count):
        forward_weights = (
            lax.all_gather(shard_weights[0], "fsdp", axis=0, tiled=True),
            lax.all_gather(shard_weights[1], "fsdp", axis=0, tiled=True),
            lax.all_gather(shard_weights[2], "fsdp", axis=0, tiled=True),
            lax.all_gather(shard_weights[3], "fsdp", axis=0, tiled=True),
            lax.all_gather(shard_weights[4], "fsdp", axis=0, tiled=True),
        )
        token_rows = block_in[micro_step, 0].astype(jnp.float32)
        result_rows, kept_values = forward_pass(token_rows, vector_params, forward_weights)
        backward_weights = (
            lax.all_gather(shard_weights[0], "fsdp", axis=0, tiled=True),
            lax.all_gather(shard_weights[1], "fsdp", axis=0, tiled=True),
            lax.all_gather(shard_weights[2], "fsdp", axis=0, tiled=True),
            lax.all_gather(shard_weights[3], "fsdp", axis=0, tiled=True),
            lax.all_gather(shard_weights[4], "fsdp", axis=0, tiled=True),
        )
        live_mask = (positions < lengths[micro_step, 0]).astype(jnp.float32)[:, None]
        seed_grad = cotangent[micro_step, 0] * live_mask
        grad_rows, vector_part, operands = backward_pass(
            seed_grad, vector_params, backward_weights, kept_values
        )
        outputs.append(result_rows)
        grads_in.append(grad_rows)
        vector_terms.append(vector_part)
        batch_terms.append(
            lax.psum_scatter(weight_terms(operands), "fsdp", scatter_dimension=0, tiled=True)
        )
    shard_grads = reduce(jnp.add, batch_terms)
    vector_grads = lax.psum(reduce(jnp.add, vector_terms), ("dp", "fsdp"))
    vec_first = BETA_ONE * vector_first + (1.0 - BETA_ONE) * vector_grads
    vec_second = BETA_TWO * vector_second + (1.0 - BETA_TWO) * vector_grads * vector_grads
    vec_new = vector_params - RATE_VECTOR * (vec_first / (1.0 - BETA_ONE**STEP)) / (
        jnp.sqrt(vec_second / (1.0 - BETA_TWO**STEP)) + EPS_ADAM
    )
    tile_side = tile_master.shape[-1]
    per_owner = tile_master.shape[1]
    all_cols = shard_grads.shape[1]
    tile_rows = shard_rows // tile_side
    tile_cols = all_cols // tile_side
    local_tiles = (
        shard_grads.reshape(tile_rows, tile_side, tile_cols, tile_side)
        .transpose(0, 2, 1, 3)
        .reshape(-1, tile_side, tile_side)
    )
    tile_count = local_tiles.shape[0]
    slot_index = slot_table(tile_owner[0], per_owner)
    slot_total = per_owner * lax.axis_size("dp")
    slot_match = slot_index[None, :] == jnp.arange(slot_total, dtype=jnp.int32)[:, None]
    source = jnp.sum(
        jnp.where(slot_match, jnp.arange(tile_count, dtype=jnp.int32)[None, :], 0), axis=1
    )
    filled = jnp.any(slot_match, axis=1)
    outgoing = jnp.where(filled[:, None, None], jnp.take(local_tiles, source, axis=0), 0.0)
    owned_grads = lax.psum_scatter(outgoing, "dp", scatter_dimension=0, tiled=True)
    master_new, first_new, second_new, stats_new, bases_new = soap_update(
        owned_grads, tile_master[0], tile_first[0], tile_second[0], tile_stats[0], tile_bases[0]
    )
    gathered = lax.all_gather(master_new.astype(jnp.bfloat16), "dp", axis=0, tiled=True)
    tiles_back = jnp.take(gathered, slot_index, axis=0)
    whole_new = (
        tiles_back.reshape(tile_rows, tile_cols, tile_side, tile_side)
        .transpose(0, 2, 1, 3)
        .reshape(shard_rows, all_cols)
    )
    w_in_new = whole_new[:, : 3 * model_width]
    w_out_new = whole_new[:, 3 * model_width : 4 * model_width]
    w_gate_new = whole_new[:, 4 * model_width : 4 * model_width + hidden_width]
    w_up_new = whole_new[:, 4 * model_width + hidden_width : 4 * model_width + 2 * hidden_width]
    w_down_new = whole_new[:, 4 * model_width + 2 * hidden_width :]
    block_out = jnp.stack(outputs, axis=0)[:, None]
    grad_in = jnp.stack(grads_in, axis=0)[:, None]
    return (
        block_out,
        grad_in,
        vec_new,
        vec_first,
        vec_second,
        w_in_new,
        w_out_new,
        w_gate_new,
        w_up_new,
        w_down_new,
        master_new[None],
        first_new[None],
        second_new[None],
        stats_new[None],
        bases_new[None],
    )


def solution(mesh):
    return jax.shard_map(
        shards,
        mesh=mesh,
        in_specs=(
            P(None, "dp", "fsdp", None),
            P(None, "dp", "fsdp", None),
            P(None, "dp"),
            P(),
            P(),
            P(),
            P("fsdp", None),
            P("fsdp", None),
            P("fsdp", None),
            P("fsdp", None),
            P("fsdp", None),
            P("fsdp", None),
            P("fsdp", "dp", None, None),
            P("fsdp", "dp", None, None),
            P("fsdp", "dp", None, None),
            P("fsdp", "dp", None, None, None),
            P("fsdp", "dp", None, None, None),
        ),
        out_specs=(
            P(None, "dp", "fsdp", None),
            P(None, "dp", "fsdp", None),
            P(),
            P(),
            P(),
            P("fsdp", None),
            P("fsdp", None),
            P("fsdp", None),
            P("fsdp", None),
            P("fsdp", None),
            P("fsdp", "dp", None, None),
            P("fsdp", "dp", None, None),
            P("fsdp", "dp", None, None),
            P("fsdp", "dp", None, None, None),
            P("fsdp", "dp", None, None, None),
        ),
        check_vma=False,
    )
```

profile of v0, /device:TPU:1, one launch (start us, length us, event | category | flops | bytes accessed | tf_op | source)
XLA Modules:
  0.0 2214.6 jit_solution(119198259347925992)
XLA Ops:
  11.5 73.7 %all-gather.7.cloned.1.call-done = bf16[1024,3072]{1,0:T(8,128)(2,1)} async-done(((bf16[128,3072]{1,0:T(8,128)(2,1)}), bf16[1024,3072]{1,0:T(8,128)(2,1)}) %all-gather.7.cloned.1.call-update) | async-done | bytes 6291472 | tf_op jit(solution)/shard_map/all_gather | solution.py:279
  85.2 4.0 fusion.73
  91.8 2.5 collective-permute-start.1
  97.0 24.9 %all-gather.9.cloned.1.call-done = bf16[1024,1024]{1,0:T(8,128)(2,1)} async-done(((bf16[128,1024]{1,0:T(8,128)(2,1)}), bf16[1024,1024]{1,0:T(8,128)(2,1)}) %all-gather.9.cloned.1.call-update) | async-done | bytes 2097168 | tf_op jit(solution)/shard_map/all_gather | solution.py:280
  121.9 3.0 multiply_reduce_fusion.10
  125.6 104.4 %all-gather.11.cloned.1.call-done = bf16[1024,4608]{1,0:T(8,128)(2,1)} async-done(((bf16[128,4608]{1,0:T(8,128)(2,1)}), bf16[1024,4608]{1,0:T(8,128)(2,1)}) %all-gather.11.cloned.1.call-update) | async-done | bytes 9437200 | tf_op jit(solution)/shard_map/all_gather | solution.py:281
  230.0 6.6 fusion.97
  236.6 95.5 %all-gather.13.cloned.1.call-done = bf16[1024,4608]{1,0:T(8,128)(2,1)} async-done(((bf16[128,4608]{1,0:T(8,128)(2,1)}), bf16[1024,4608]{1,0:T(8,128)(2,1)}) %all-gather.13.cloned.1.call-update) | async-done | bytes 9437200 | tf_op jit(solution)/shard_map/all_gather | solution.py:282
  332.0 6.6 fusion.98
  338.6 95.5 %all-gather.15.cloned.1.call-done = bf16[1024,4608]{1,0:T(8,128)(2,1)} async-done(((bf16[128,4608]{1,0:T(8,128)(2,1)}), bf16[1024,4608]{1,0:T(8,128)(2,1)}) %all-gather.15.cloned.1.call-update) | async-done | bytes 9437200 | tf_op jit(solution)/shard_map/all_gather | solution.py:283
  434.1 8.5 multiply_convert_fusion.2
  442.6 8.4 fusion.101
  451.1 5.7 multiply_reduce_fusion.7
  456.8 2.8 fusion.99
  459.7 2.8 fusion.100
  462.5 5.6 multiply_convert_fusion
  468.2 5.6 fusion.102
  473.7 5.0 multiply_reduce_fusion.3
  486.6 3.7 collective-permute-done.3
  490.9 6.5 convolution_dynamic-update-slice_fusion.7
  497.4 2.9 convolution_dynamic-update-slice_fusion.9
  500.3 8.0 convolution_dynamic-update-slice_fusion.5
  508.3 7.9 convolution_dynamic-update-slice_fusion.4
  516.3 6.6 convolution_dynamic-update-slice_fusion.6
  522.9 2.8 convolution_dynamic-update-slice_fusion.8
  525.7 7.9 convolution_dynamic-update-slice_fusion.2
  533.6 7.9 convolution_dynamic-update-slice_fusion.1
  541.5 8.0 convolution_dynamic-update-slice_fusion.3
  549.6 8.0 convolution_dynamic-update-slice_fusion
  557.6 71.2 %add.286 = f32[1024,17920]{1,0:T(8,128)} add(f32[1024,17920]{1,0:T(8,128)} %convolution_dynamic-update-slice_fusion.3, f32[1024,17920]{1,0:T(8,128)} %convolution_dynamic-update-slice_fusion) | non-fusion elementwise | flops 18350080 | bytes 220200960 | tf_op jit(solution)/shard_map/add | solution.py:305
  629.9 703.9 %reduce-scatter.5.cloned.1.call-done = f32[128,17920]{1,0:T(8,128)} async-done(((f32[1024,17920]{1,0:T(8,128)}), f32[128,17920]{1,0:T(8,128)}) %reduce-scatter.5.cloned.1.call-update) | async-done | bytes 9175056 | tf_op jit(solution)/shard_map/reduce_scatter | solution.py:303
  1333.8 9.5 copy.137
  1343.4 9.5 copy.138
  1352.9 14.3 gather_fusion
  1367.3 11.4 select_select_fusion
  1380.6 118.5 %reduce-scatter.3.cloned.1.call-done = f32[12,128,128]{2,1,0:T(8,128)} async-done(((f32[192,128,128]{2,1,0:T(8,128)}), f32[12,128,128]{2,1,0:T(8,128)}) %reduce-scatter.3.cloned.1.call-update) | async-done | bytes 786448 | tf_op jit(solution)/shard_map/reduce_scatter | solution.py:331
  1499.2 2.7 fusion.24
  1501.9 2.1 fusion.8
  1507.4 2.8 fusion.96
  1510.3 2.8 copy.183
  1513.8 6.9 fusion.6
  1520.7 6.9 fusion.7
  1528.8 2.2 fusion.60
  1531.4 3.7 fusion.51
  1535.9 78.0 %psum.7 = f32[5,1024]{1,0:T(8,128)S(1)} all-reduce(f32[5,1024]{1,0:T(8,128)S(1)} %add.260), channel_id=1, replica_groups=mesh['dp'=16,'fsdp'=8] {'dp','fsdp'}, use_global_device_ids=true, to_apply=%region_18.19 | all-reduce | flops 5120 | bytes 40960 | tf_op jit(solution)/shard_map/psum | solution.py:306
  1615.3 1.8 fusion.50
  1620.4 1.8 fusion.2
  1624.4 2.3 fusion.103
  1626.7 2.3 copy.150
  1629.0 2.3 fusion.14
  1631.4 142.3 %custom-call.8 = f32[12,128,128]{2,1,0:T(8,128)} custom-call(f32[12,128,128]{2,1,0:T(8,128)} %fusion.14), custom_call_target="Cholesky" | custom-call | tf_op jit(solution)/shard_map/jit(cholesky)/cholesky | solution.py:210
  1773.7 2.0 fusion.26
  1779.2 2.1 fusion.11
  1781.3 142.1 %custom-call.10 = f32[12,128,128]{2,1,0:T(8,128)} custom-call(f32[12,128,128]{2,1,0:T(8,128)} %fusion.11), custom_call_target="Cholesky" | custom-call | tf_op jit(solution)/shard_map/jit(cholesky)/cholesky | solution.py:210
  1925.0 2.5 select_bitcast_fusion.1
  1927.6 118.7 %custom-call.11 = f32[12,1,128,128]{2,3,1,0:T(8,128)S(1)} custom-call(f32[12,1,128,128]{3,2,1,0:T(8,128)} %get-tuple-element.146), custom_call_target="InvertDiagBlocksLowerTriangular" | custom-call | tf_op jit(solution)/shard_map/vmap(jit(_solve_triangular))/triangular_solve | solution.py:205
  2046.2 119.6 %custom-call.9 = f32[12,1,128,128]{2,3,1,0:T(8,128)} custom-call(f32[12,1,128,128]{3,2,1,0:T(8,128)} %get-tuple-element.145), custom_call_target="InvertDiagBlocksLowerTriangular" | custom-call | tf_op jit(solution)/shard_map/vmap(jit(_solve_triangular))/triangular_solve | solution.py:205
  2171.5 10.3 gather_fusion.1
  2181.8 4.9 fusion
  2186.7 6.6 copy.146
  2193.3 2.1 slice.203
  2197.0 2.2 fusion.93
  2199.2 2.3 copy.159
  2201.5 1.8 copy.160
  (284 shorter events, 50.7 us)
Async XLA Ops:
  7.2 4.1 copy-start.3
  7.2 78.0 %all-gather.7.cloned.1.call-start = ((), (), s32[]{:S(2)}) async-start(), calls=%async_computation.2 | async-start | bytes 7077888 | tf_op jit(solution)/shard_map/all_gather | solution.py:279
  7.9 114.0 %all-gather.9.cloned.1.call-start = ((), (), s32[]{:S(2)}) async-start(), calls=%async_computation.3 | async-start | bytes 2359296 | tf_op jit(solution)/shard_map/all_gather | solution.py:280
  8.7 221.3 %all-gather.11.cloned.1.call-start = ((), (), s32[]{:S(2)}) async-start(), calls=%async_computation.4 | async-start | bytes 10616832 | tf_op jit(solution)/shard_map/all_gather | solution.py:281
  9.4 322.6 %all-gather.13.cloned.1.call-start = ((), (), s32[]{:S(2)}) async-start(), calls=%async_computation.5 | async-start | bytes 10616832 | tf_op jit(solution)/shard_map/all_gather | solution.py:282
  10.0 424.1 %all-gather.15.cloned.1.call-start = ((), (), s32[]{:S(2)}) async-start(), calls=%async_computation.6 | async-start | bytes 10616832 | tf_op jit(solution)/shard_map/all_gather | solution.py:283
  10.6 1323.3 %reduce-scatter.5.cloned.1.call-start = ((), (), s32[]{:S(2)}) async-start(), calls=%async_computation.9 | async-start | bytes 82575360 | tf_op jit(solution)/shard_map/reduce_scatter | solution.py:303
  11.4 479.4 %copy-start.77 = (f32[128]{0:T(128)}, f32[128]{0:T(128)S(1)}, u32[]{:S(2)}) copy-start(f32[128]{0:T(128)S(1)} %add_rsqrt_fusion.3) | copy-start | bytes 1540
  11.5 504.8 %copy-start.79 = (f32[128]{0:T(128)}, f32[128]{0:T(128)S(1)}, u32[]{:S(2)}) copy-start(f32[128]{0:T(128)S(1)} %add_rsqrt_fusion.1) | copy-start | bytes 1540
  11.5 504.7 %copy-start.48 = (f32[1,1024]{1,0:T(1,128)}, f32[1,1024]{1,0:T(1,128)S(1)}, u32[]{:S(2)}) copy-start(f32[1,1024]{1,0:T(1,128)S(1)} %get-tuple-element.144) | copy-start | bytes 12292
  85.2 5.4 copy-start
  89.2 6.5 copy-start.6
  89.3 6.4 copy-start.24
  89.3 6.3 collective-permute-start
  91.7 4.0 copy-start.8
  91.8 3.9 collective-permute-start.1
  97.0 27.9 %copy-start.41 = (bf16[128,1024]{1,0:T(8,128)(2,1)}, bf16[128,1024]{1,0:T(8,128)(2,1)S(1)}, u32[]{:S(2)}) copy-start(bf16[128,1024]{1,0:T(8,128)(2,1)S(1)} %get-tuple-element.149) | copy-start | bytes 786436
  97.0 28.4 %copy-start.43 = (bf16[128,1024]{1,0:T(8,128)(2,1)}, bf16[128,1024]{1,0:T(8,128)(2,1)S(1)}, u32[]{:S(2)}) copy-start(bf16[128,1024]{1,0:T(8,128)(2,1)S(1)} %get-tuple-element.121) | copy-start | bytes 786436
  125.5 111.1 %copy-start.12 = (f32[128,1024]{1,0:T(8,128)}, f32[128,1024]{1,0:T(8,128)S(1)}, u32[]{:S(2)}) copy-start(f32[128,1024]{1,0:T(8,128)S(1)} %get-tuple-element.155) | copy-start | bytes 1572868
  332.0 119.0 %slice-start.3 = ((s8[9437184]{0:T(1024)(128)(4,1)}), s8[1048576]{0:T(1024)(128)(4,1)S(1)}, s32[]{:S(2)}) async-start(s8[9437184]{0:T(1024)(128)(4,1)} %bitcast.242), calls=%async_computation.13 | async-start | bytes 2097152
  434.1 17.0 slice-start.4
  434.1 17.0 slice-start.5
  442.6 8.5 copy-start.32
  442.6 8.5 copy-start.26
  442.6 8.5 copy-start.10
  442.6 8.5 copy-start.13
  442.6 14.2 slice-start
  442.6 14.2 slice-start.1
  451.1 5.7 slice-start.2
  456.8 5.7 slice-start.8
  456.8 5.7 slice-start.9
  468.1 5.6 copy-start.34
  473.7 5.0 copy-start.37
  473.7 5.0 copy-start.45
  479.2 18.3 copy-start.17
  479.2 43.7 %copy-start.19 = (f32[128,1024]{1,0:T(8,128)}, f32[128,1024]{1,0:T(8,128)S(1)}, u32[]{:S(2)}) copy-start(f32[128,1024]{1,0:T(8,128)S(1)} %get-tuple-element.135) | copy-start | bytes 1572868
  482.1 8.8 copy-start.56
  482.1 4.5 collective-permute-start.2
  485.1 31.1 %copy-start.58 = (bf16[128,1024]{1,0:T(8,128)(2,1)}, bf16[128,1024]{1,0:T(8,128)(2,1)S(1)}, u32[]{:S(2)}) copy-start(bf16[128,1024]{1,0:T(8,128)(2,1)S(1)} %get-tuple-element.139) | copy-start | bytes 786436
  485.1 5.7 copy-start.4
  485.1 5.1 collective-permute-start.3
  490.7 6.7 copy-start.50
  490.8 25.5 %copy-start.54 = (bf16[128,1024]{1,0:T(8,128)(2,1)}, bf16[128,1024]{1,0:T(8,128)(2,1)S(1)}, u32[]{:S(2)}) copy-start(bf16[128,1024]{1,0:T(8,128)(2,1)S(1)} %multiply_convert_fusion.6) | copy-start | bytes 786436
  490.8 6.6 copy-start.52
  490.9 6.5 copy-start.44
  500.3 8.0 copy-start.27
  516.2 6.7 copy-start.42
  525.7 7.9 copy-start.35
  533.6 7.9 copy-start.28
  541.5 8.0 copy-start.30
  628.8 870.4 %reduce-scatter.3.cloned.1.call-start = ((), (), s32[]{:S(2)}) async-start(), calls=%async_computation.7 | async-start | bytes 13369344 | tf_op jit(solution)/shard_map/reduce_scatter | solution.py:331
  1378.7 792.8 %all-gather.17.cloned.1.call-start = ((), (), s32[]{:S(2)}) async-start(), calls=%async_computation.8 | async-start | bytes 6684672 | tf_op jit(solution)/shard_map/all_gather | solution.py:335
  1499.2 4.8 copy-start.1
  1499.2 4.8 copy-start.39
  1513.7 7.0 copy-start.14
  1513.7 7.0 copy-start.29
  1513.8 15.0 slice-start.6
  1520.7 8.0 slice-start.7
  1520.7 8.0 copy-start.55
  1520.7 8.0 copy-start.59
  1531.4 83.9 %copy-start.18 = (f32[128,1024]{1,0:T(8,128)S(1)}, f32[128,1024]{1,0:T(8,128)}, u32[]{:S(2)}) copy-start(f32[128,1024]{1,0:T(8,128)} %copy-done.17) | copy-start | bytes 1572868
  1778.1 145.4 %copy-start.38 = (f32[12,128,128]{2,1,0:T(8,128)S(1)}, f32[12,128,128]{2,1,0:T(8,128)}, u32[]{:S(2)}) copy-start(f32[12,128,128]{2,1,0:T(8,128)} %custom-call.8) | copy-start | bytes 2359300
  1923.5 242.3 %copy-start.16 = (f32[12,128,128]{2,1,0:T(8,128)S(1)}, f32[12,128,128]{2,1,0:T(8,128)}, u32[]{:S(2)}) copy-start(f32[12,128,128]{2,1,0:T(8,128)} %copy-done.15) | copy-start | bytes 2359300
  2171.5 10.3 copy-start.81
  (42 other events, 118.1 us)
Sparse Core Ops, SparseCore 0:
  9.7 75.4 all-gather.6
  86.9 35.0 all-gather.8
  123.6 106.3 all-gather.10
  231.5 100.4 all-gather.12
  333.5 100.4 all-gather.14
  629.0 704.8 reduce-scatter.4
  1378.8 120.3 reduce-scatter.2
  1510.4 64.3 all-gather.16
where the time goes:
time: 2220 us; the launch traced here: 2210 us
  waiting for transfers between devices  1220 us (55%)
  other arithmetic  633 us (29%)
  matrix products  178 us (8%)
  local copies, waits for them, and re-layouts  79.6 us (4%)
  blocking collectives  78 us (4%)
    reduce_scatter x1, waiting for transfers between devices, shards(): lax.psum_scatter(weight_terms(operands), 'fsdp', scatter_dimension=0, til...  704 us
    another operation x6, other arithmetic, orthonormal(): lower_factor = jnp.linalg.cholesky(gram)  286 us
    another operation x4, other arithmetic, solve_lower(): jax.scipy.linalg.solve_triangular(lower_factor, rhs_matrix, lower=True)  241 us
    reduce_scatter x1, waiting for transfers between devices, shards(): lax.psum_scatter(outgoing, 'dp', scatter_dimension=0, tiled=True)  119 us
    all_gather x1, waiting for transfers between devices, shards(): lax.all_gather(shard_weights[2], 'fsdp', axis=0, tiled=True)  104 us
    all_gather x1, waiting for transfers between devices, shards(): lax.all_gather(shard_weights[4], 'fsdp', axis=0, tiled=True)  95.5 us
    all_gather x1, waiting for transfers between devices, shards(): lax.all_gather(shard_weights[3], 'fsdp', axis=0, tiled=True)  95.5 us
    psum x1, blocking collectives, shards(): vector_grads = lax.psum(reduce(jnp.add, vector_terms), ('dp', 'fsdp'))  78 us
  transfers between devices with their start and end apart: 12, of which 8 were waited for; matrix products, arithmetic and copies ran while one was open for 28% of the time, Pallas kernels for 0%

commit v1 on v0

v1 whole, which is shorter than its diff:
```python
import functools

import jax
import jax.numpy as jnp
from jax import lax
from jax.experimental import pallas as pl
from jax.experimental.pallas import tpu as pltpu
from jax.sharding import PartitionSpec as P

STEP = 10


EPS_NORM = 1e-05
EPS_ADAM = 1e-08
BETA_ONE = 0.5
BETA_TWO = 0.5
BETA_STAT = 0.5
RATE_MATRIX = 0.03
RATE_VECTOR = 0.2
DECAY_WEIGHT = 0.01
PRECISE = lax.Precision.HIGHEST
BACK_DIMS = (((1,), (1,)), ((), ()))
TOKEN_DIMS = (((0,), (0,)), ((), ()))

PANEL = 32


def from_behind(value, axis, by):
    length = lax.axis_size(axis)
    pairs = [(i, i + by) for i in range(length) if 0 <= i + by < length]
    return lax.ppermute(value, axis, pairs)


def flip(value, axis, bit):
    length = lax.axis_size(axis)
    return lax.ppermute(value, axis, [(i, i ^ bit) for i in range(length)])


def sum_all(value):
    for axis, bit in (("dp", 1), ("fsdp", 1), ("fsdp", 2), ("fsdp", 4), ("dp", 2), ("dp", 4), ("dp", 8)):
        value = value + flip(value, axis, bit)
    return value


def rms_factor(values):
    return lax.rsqrt(jnp.mean(values * values, axis=-1, keepdims=True) + EPS_NORM)


def norm_back(values, scale_val, gain_row, grad_out):
    weighted = grad_out * gain_row
    inner = jnp.mean(values * weighted, axis=-1, keepdims=True)
    grad_values = scale_val * weighted - values * scale_val * scale_val * scale_val * inner
    grad_gain = jnp.sum(values * scale_val * grad_out, axis=0)
    return (grad_values, grad_gain)


def outer_sum(left_arr, right_arr):
    return lax.dot_general(left_arr, right_arr, TOKEN_DIMS, preferred_element_type=jnp.float32)


def back_dot(left_arr, right_arr):
    return lax.dot_general(left_arr, right_arr, BACK_DIMS, preferred_element_type=jnp.float32)


def exchange(value, axis, groups=None):
    return lax.all_to_all(value, axis, 0, 0, axis_index_groups=groups)


def token_scatter(partial_rows):
    parts = lax.axis_size("fsdp")
    cut = partial_rows.astype(jnp.bfloat16).reshape(parts, -1, partial_rows.shape[1])
    return jnp.sum(exchange(cut, "fsdp").astype(jnp.float32), axis=0)


def to_columns(shard):
    parts = lax.axis_size("fsdp")
    rows, width = shard.shape
    cut = shard.reshape(rows, parts, width // parts).transpose(1, 0, 2)
    return exchange(cut, "fsdp").reshape(parts * rows, width // parts)


def chip_sum(value, core):
    parts = lax.axis_size("fsdp")
    half = value.shape[0] // parts // 2
    cut = value.reshape(parts, 2, half, value.shape[1])
    mine = lax.dynamic_index_in_dim(cut, core, 1, keepdims=False)
    other = lax.dynamic_index_in_dim(cut, 1 - core, 1, keepdims=False)
    return mine + flip(other.astype(jnp.bfloat16), "dp", 1).astype(jnp.float32)


def slot_table(owner_row, per_owner):
    tile_count = owner_row.shape[0]
    same_owner = owner_row[None, :] == owner_row[:, None]
    before = (
        jnp.arange(tile_count, dtype=jnp.int32)[None, :]
        < jnp.arange(tile_count, dtype=jnp.int32)[:, None]
    )
    slot_rank = jnp.sum((same_owner & before).astype(jnp.int32), axis=1)
    return owner_row * per_owner + slot_rank


def rotate_into(left_basis, matrix, right_basis):
    step_one = jnp.einsum("sji,sjk->sik", left_basis, matrix, precision=PRECISE)
    return jnp.einsum("sik,skl->sil", step_one, right_basis, precision=PRECISE)


def rotate_back(left_basis, matrix, right_basis):
    step_one = jnp.einsum("sij,sjk->sik", left_basis, matrix, precision=PRECISE)
    return jnp.einsum("sik,slk->sil", step_one, right_basis, precision=PRECISE)


def orthonormal_kernel(m_ref, q_ref, w_ref):
    count, side = m_ref.shape[0], m_ref.shape[1]
    shape = (PANEL, side)
    rows = lax.broadcasted_iota(jnp.int32, shape, 0)
    lanes = lax.broadcasted_iota(jnp.int32, shape, 1)
    all_rows = lax.broadcasted_iota(jnp.int32, (side, side), 0)
    all_lanes = lax.broadcasted_iota(jnp.int32, (side, side), 1)
    for g in range(count):
        w_ref[g] = lax.dot_general(
            m_ref[g], m_ref[g], TOKEN_DIMS, precision=PRECISE, preferred_element_type=jnp.float32
        )

    def block(b, carry):
        base = pl.multiple_of(b * PANEL, PANEL)
        panels = [w_ref[g, pl.ds(base, PANEL), :] for g in range(count)]
        pivots = [jnp.zeros(shape, jnp.float32)] * count
        for k in range(PANEL):
            first = (k // 8) * 8
            row, lane = rows[first:], lanes[first:]
            copies = (PANEL - first) // 8
            for g in range(count):
                part = panels[g][first:]
                column = jnp.broadcast_to(part[:, k : k + 1], part.shape)
                pivot = jnp.broadcast_to(column[k - first : k - first + 1], (8, side))
                top = jnp.broadcast_to(part[k - first : k - first + 1], (8, side))
                top = jnp.where(lane[:8] == k, 1.0, top)
                scaled = jnp.concatenate([top / pivot] * copies, 0)
                kept = jnp.where((lane == k) & (row > k), 0.0, part)
                part = kept - jnp.where(row > k, column, 0.0) * scaled
                part = jnp.where(row == k, jnp.concatenate([top] * copies, 0), part)
                panels[g] = jnp.concatenate([panels[g][:first], part], 0) if first else part
                pivots[g] = jnp.where(rows == k, jnp.concatenate([pivot] * (PANEL // 8), 0), pivots[g])
        below = all_rows >= base + PANEL
        for g in range(count):
            done = panels[g] * lax.rsqrt(pivots[g])
            coef = jnp.where((lanes >= PANEL) & (lanes < side - base), done, 0.0)
            source = jnp.where((lanes < PANEL) & (lanes > rows), 0.0, done)
            change = lax.dot_general(
                coef, source, TOKEN_DIMS, precision=PRECISE, preferred_element_type=jnp.float32
            )
            change = pltpu.roll(change, base, 0)
            kept = jnp.where(below & (all_lanes < PANEL), 0.0, w_ref[g])
            w_ref[g] = kept - jnp.where(below, change, 0.0)
            w_ref[g, pl.ds(base, PANEL), :] = done
            w_ref[g] = pltpu.roll(w_ref[g], side - PANEL, 1)
        return carry

    lax.fori_loop(0, side // PANEL, block, 0)
    for g in range(count):
        inverse = jnp.where(all_lanes <= all_rows, w_ref[g], 0.0)
        q_ref[g] = lax.dot_general(
            m_ref[g], inverse, BACK_DIMS, precision=PRECISE, preferred_element_type=jnp.float32
        )


def orthonormal(matrix):
    return pl.pallas_call(
        orthonormal_kernel,
        out_shape=jax.ShapeDtypeStruct(matrix.shape, jnp.float32),
        in_specs=[pl.BlockSpec(memory_space=pltpu.VMEM)],
        out_specs=pl.BlockSpec(memory_space=pltpu.VMEM),
        scratch_shapes=[pltpu.VMEM(matrix.shape, jnp.float32)],
        compiler_params=pltpu.CompilerParams(vmem_limit_bytes=32 * 2**20),
    )(matrix)


def soap_update(grad_tiles, master, first, second, stats, bases):
    left_basis = bases[:, 0]
    right_basis = bases[:, 1]
    rotated = rotate_into(left_basis, grad_tiles, right_basis)
    first_new = BETA_ONE * first + (1.0 - BETA_ONE) * grad_tiles
    second_new = BETA_TWO * second + (1.0 - BETA_TWO) * rotated * rotated
    moment_rot = rotate_into(left_basis, first_new, right_basis)
    direction = (
        moment_rot
        / (1.0 - BETA_ONE**STEP)
        / (jnp.sqrt(second_new / (1.0 - BETA_TWO**STEP)) + EPS_ADAM)
    )
    master_new = master - RATE_MATRIX * (
        rotate_back(left_basis, direction, right_basis) + DECAY_WEIGHT * master
    )
    stat_left = BETA_STAT * stats[:, 0] + (1.0 - BETA_STAT) * jnp.einsum(
        "sik,sjk->sij", grad_tiles, grad_tiles, precision=PRECISE
    )
    stat_right = BETA_STAT * stats[:, 1] + (1.0 - BETA_STAT) * jnp.einsum(
        "ski,skj->sij", grad_tiles, grad_tiles, precision=PRECISE
    )
    stats_new = jnp.stack([stat_left, stat_right], axis=1)
    turned = jnp.einsum("stij,stjk->stik", stats_new, bases, precision=PRECISE)
    bases_new = orthonormal(turned.reshape((-1,) + turned.shape[2:])).reshape(bases.shape)
    return (master_new, first_new, second_new, stats_new, bases_new)


def shards(
    block_in,
    cotangent,
    lengths,
    vector_params,
    vector_first,
    vector_second,
    w_in,
    w_out,
    w_gate,
    w_up,
    w_down,
    tile_owner,
    tile_master,
    tile_first,
    tile_second,
    tile_stats,
    tile_bases,
):
    micro_count, _, tok_count, model_width = block_in.shape
    hidden_width = w_gate.shape[1]
    parts = lax.axis_size("fsdp")
    core = lax.axis_index("dp") % 2
    g_one, g_two, k_zero, k_one, k_two = [vector_params[i] for i in range(5)]

    whole_in = lax.all_gather(w_in, "fsdp", axis=0, tiled=True)
    whole_out = lax.all_gather(w_out, "fsdp", axis=0, tiled=True)
    positions = lax.axis_index("fsdp") * tok_count + jnp.arange(tok_count, dtype=jnp.int32)
    live_mask = (positions[None, :] < lengths).astype(jnp.float32)[:, :, None]
    seed_grad = (cotangent[:, 0] * live_mask).reshape(-1, model_width)
    grad_feed = lax.all_gather(seed_grad.astype(jnp.bfloat16), "fsdp", axis=0, tiled=True)
    gate_cols = to_columns(w_gate)
    up_cols = to_columns(w_up)
    down_cols = to_columns(w_down)

    token_rows = block_in.astype(jnp.float32).reshape(-1, model_width)
    scale_one = rms_factor(token_rows)
    normed = (token_rows * scale_one * g_one).astype(jnp.bfloat16)
    mixed_all = jnp.dot(normed, whole_in, preferred_element_type=jnp.float32)
    part_b = mixed_all[:, :model_width]
    part_c = mixed_all[:, model_width : 2 * model_width]
    part_x = mixed_all[:, 2 * model_width :]
    product = (part_b * part_x).reshape(micro_count, tok_count, model_width)
    extended = jnp.concatenate([from_behind(product[:, -2:], "fsdp", 1), product], axis=1)
    convolved = (
        k_zero * extended[:, :-2] + k_one * extended[:, 1:-1] + k_two * extended[:, 2:]
    ).reshape(-1, model_width)
    gated_conv = (part_c * convolved).astype(jnp.bfloat16)
    residual = token_rows + jnp.dot(gated_conv, whole_out, preferred_element_type=jnp.float32)
    scale_two = rms_factor(residual)
    normed_two = (residual * scale_two * g_two).astype(jnp.bfloat16)

    fed = lax.all_gather(normed_two, "fsdp", axis=0, tiled=True)
    gate_val = jnp.dot(fed, gate_cols, preferred_element_type=jnp.float32)
    up_val = jnp.dot(fed, up_cols, preferred_element_type=jnp.float32)
    sigmoid_gate = jax.nn.sigmoid(gate_val)
    activation = (gate_val * sigmoid_gate * up_val).astype(jnp.bfloat16)
    grad_act = jnp.dot(grad_feed, down_cols, preferred_element_type=jnp.float32)
    grad_gate = (grad_act * up_val * sigmoid_gate * (1.0 + gate_val * (1.0 - sigmoid_gate))).astype(
        jnp.bfloat16
    )
    grad_up = (grad_act * gate_val * sigmoid_gate).astype(jnp.bfloat16)
    grad_normed_two = token_scatter(back_dot(grad_gate, gate_cols) + back_dot(grad_up, up_cols))
    result_rows = residual + lax.psum_scatter(
        back_dot(activation, down_cols).astype(jnp.bfloat16), "fsdp", scatter_dimension=0, tiled=True
    ).astype(jnp.float32)
    feed_grads = jnp.concatenate(
        [outer_sum(fed, grad_gate), outer_sum(fed, grad_up), outer_sum(grad_feed, activation)], axis=1
    )
    feed_half = exchange(chip_sum(feed_grads, core).astype(jnp.bfloat16), "fsdp")
    half_rows = feed_half.shape[1]
    feed_half = (
        feed_half.reshape(parts, half_rows, 3, -1).transpose(1, 2, 0, 3).reshape(half_rows, 3 * hidden_width)
    )

    grad_res_norm, grad_gain_two = norm_back(residual, scale_two, g_two, grad_normed_two)
    grad_resid = seed_grad + grad_res_norm
    grad_branch = grad_resid.astype(jnp.bfloat16)
    grad_gated = back_dot(grad_branch, whole_out)
    grad_part_c = grad_gated * convolved
    grad_conv = (grad_gated * part_c).reshape(micro_count, tok_count, model_width)
    grad_ext = jnp.concatenate([grad_conv, from_behind(grad_conv[:, :2], "fsdp", -1)], axis=1)
    grad_product = (
        k_two * grad_conv + k_one * grad_ext[:, 1 : tok_count + 1] + k_zero * grad_ext[:, 2:]
    ).reshape(-1, model_width)
    grad_kernel = jnp.stack(
        [
            jnp.sum(grad_conv * extended[:, :-2], axis=(0, 1)),
            jnp.sum(grad_conv * extended[:, 1:-1], axis=(0, 1)),
            jnp.sum(grad_conv * extended[:, 2:], axis=(0, 1)),
        ]
    )
    grad_mixed = jnp.concatenate(
        [grad_product * part_x, grad_part_c, grad_product * part_b], axis=1
    ).astype(jnp.bfloat16)
    conv_grads = jnp.concatenate([outer_sum(normed, grad_mixed), outer_sum(gated_conv, grad_branch)], axis=1)
    conv_half = exchange(chip_sum(conv_grads, core).astype(jnp.bfloat16), "fsdp")
    conv_half = jnp.sum(conv_half.astype(jnp.float32), axis=0).astype(jnp.bfloat16)
    grad_normed = back_dot(grad_mixed, whole_in)
    grad_rows_norm, grad_gain_one = norm_back(token_rows, scale_one, g_one, grad_normed)
    grad_rows = grad_resid + grad_rows_norm

    vector_grads = sum_all(
        jnp.concatenate([grad_gain_one[None], grad_gain_two[None], grad_kernel], axis=0)
    )
    vec_first = BETA_ONE * vector_first + (1.0 - BETA_ONE) * vector_grads
    vec_second = BETA_TWO * vector_second + (1.0 - BETA_TWO) * vector_grads * vector_grads
    vec_new = vector_params - RATE_VECTOR * (vec_first / (1.0 - BETA_ONE**STEP)) / (
        jnp.sqrt(vec_second / (1.0 - BETA_TWO**STEP)) + EPS_ADAM
    )

    tile_side = tile_master.shape[-1]
    per_owner = tile_master.shape[1]
    owners = lax.axis_size("dp")
    half_grads = jnp.concatenate([conv_half, feed_half], axis=1)
    all_cols = half_grads.shape[1]
    tile_cols = all_cols // tile_side
    half_tiles = half_grads.reshape(half_rows, tile_cols, tile_side).transpose(1, 0, 2)
    slot_index = slot_table(tile_owner[0], per_owner)
    slot_match = slot_index[None, :] == jnp.arange(per_owner * owners, dtype=jnp.int32)[:, None]
    source = jnp.sum(
        jnp.where(slot_match, jnp.arange(tile_cols, dtype=jnp.int32)[None, :], 0), axis=1
    )
    filled = jnp.any(slot_match, axis=1)
    outgoing = jnp.where(
        filled[:, None, None], jnp.take(half_tiles, source, axis=0), jnp.zeros((), jnp.bfloat16)
    )
    chips = owners // 2
    same_core = [[2 * i + c for i in range(chips)] for c in range(2)]
    arrived = exchange(
        outgoing.reshape(chips, 2 * per_owner, half_rows, tile_side), "dp", same_core
    )
    chip_slots = jnp.sum(arrived.astype(jnp.float32), axis=0).reshape(
        2, per_owner, half_rows, tile_side
    )
    mine = lax.dynamic_index_in_dim(chip_slots, core, 0, keepdims=False)
    theirs = flip(lax.dynamic_index_in_dim(chip_slots, 1 - core, 0, keepdims=False), "dp", 1)
    owned_grads = jnp.where(
        core == 0,
        jnp.concatenate([mine, theirs], axis=1),
        jnp.concatenate([theirs, mine], axis=1),
    )
    master_new, first_new, second_new, stats_new, bases_new = soap_update(
        owned_grads, tile_master[0], tile_first[0], tile_second[0], tile_stats[0], tile_bases[0]
    )
    gathered = lax.all_gather(master_new.astype(jnp.bfloat16), "dp", axis=0, tiled=True)
    tiles_back = jnp.take(gathered, slot_index, axis=0)
    whole_new = tiles_back.transpose(1, 0, 2).reshape(tile_side, all_cols)
    w_in_new = whole_new[:, : 3 * model_width]
    w_out_new = whole_new[:, 3 * model_width : 4 * model_width]
    w_gate_new = whole_new[:, 4 * model_width : 4 * model_width + hidden_width]
    w_up_new = whole_new[:, 4 * model_width + hidden_width : 4 * model_width + 2 * hidden_width]
    w_down_new = whole_new[:, 4 * model_width + 2 * hidden_width :]
    whole_shape = (micro_count, 1, tok_count, model_width)
    return (
        result_rows.reshape(whole_shape),
        grad_rows.reshape(whole_shape),
        vec_new,
        vec_first,
        vec_second,
        w_in_new,
        w_out_new,
        w_gate_new,
        w_up_new,
        w_down_new,
        master_new[None],
        first_new[None],
        second_new[None],
        stats_new[None],
        bases_new[None],
    )


def solution(mesh):
    return jax.shard_map(
        shards,
        mesh=mesh,
        in_specs=(
            P(None, "dp", "fsdp", None),
            P(None, "dp", "fsdp", None),
            P(None, "dp"),
            P(),
            P(),
            P(),
            P("fsdp", None),
            P("fsdp", None),
            P("fsdp", None),
            P("fsdp", None),
            P("fsdp", None),
            P("fsdp", None),
            P("fsdp", "dp", None, None),
            P("fsdp", "dp", None, None),
            P("fsdp", "dp", None, None),
            P("fsdp", "dp", None, None, None),
            P("fsdp", "dp", None, None, None),
        ),
        out_specs=(
            P(None, "dp", "fsdp", None),
            P(None, "dp", "fsdp", None),
            P(),
            P(),
            P(),
            P("fsdp", None),
            P("fsdp", None),
            P("fsdp", None),
            P("fsdp", None),
            P("fsdp", None),
            P("fsdp", "dp", None, None),
            P("fsdp", "dp", None, None),
            P("fsdp", "dp", None, None),
            P("fsdp", "dp", None, None, None),
            P("fsdp", "dp", None, None, None),
        ),
        check_vma=False,
    )
```

time: 2220 us -> 765 us (0.34)
  waiting for transfers between devices: 1220 us -> 367 us
  other arithmetic: 633 us -> 55.2 us
  matrix products: 178 us -> 95.1 us
  starting transfers between devices: 7.23 us -> 56.1 us
  Pallas kernels: 0 us -> 38.5 us
  blocking collectives: 78 us -> 45.4 us
    reduce_scatter x2 -> x1, waiting for transfers between devices: 822 us -> 17.8 us  [shards(): lax.psum_scatter(back_dot(activation, down_cols).astype(jnp.bfloat16), 'f...]
    another operation x14 -> x2, other arithmetic: 529 us -> 0.74 us  [the longest x1 0.37 us: soap_update(): stats_new = jnp.stack([stat_left, stat_right], axis=1)]
    all_gather x5 -> x4, waiting for transfers between devices: 394 us -> 173 us  [the longest x1 73 us: shards(): whole_in = lax.all_gather(w_in, 'fsdp', axis=0, tiled=True)]
    all_to_all x0 -> x6, waiting for transfers between devices: none -> 155 us  [exchange(): return lax.all_to_all(value, axis, 0, 0, axis_index_groups=groups)]
    psum x1 -> x0, blocking collectives: 78 us -> none  [shards(): vector_grads = lax.psum(reduce(jnp.add, vector_terms), ('dp', 'fsdp'))]
    add x3 -> x12, other arithmetic: 71.6 us -> 6.21 us  [the longest x1 3.18 us: shards(): grad_resid = seed_grad + grad_res_norm]
    all_to_all x0 -> x1, blocking collectives: none -> 45.4 us  [exchange(): return lax.all_to_all(value, axis, 0, 0, axis_index_groups=groups)]
    dot_general x10 -> x5, matrix products: 66.6 us -> 25 us  [outer_sum(): lax.dot_general(left_arr, right_arr, TOKEN_DIMS, preferred_element_type=j...]
  transfers between devices with their start and end apart: 12 -> 24, of which waited for: 8 -> 20; matrix products, arithmetic and copies ran while one was open for 28% -> 17% of each run, Pallas kernels for 0% -> 5%
where the time goes in v1:
time: 765 us; the launch traced here: 753 us
  waiting for transfers between devices  367 us (48%)
  matrix products  95.1 us (12%)
  local copies, waits for them, and re-layouts  80.7 us (11%)
  starting transfers between devices  56.1 us (7%)
  other arithmetic  55.2 us (7%)
  blocking collectives  45.4 us (6%)
  Pallas kernels  38.5 us (5%)
  between operations  15 us (2%)
    all_to_all x6, waiting for transfers between devices, exchange(): return lax.all_to_all(value, axis, 0, 0, axis_index_groups=groups)  155 us
    all_gather x1, waiting for transfers between devices, shards(): whole_in = lax.all_gather(w_in, 'fsdp', axis=0, tiled=True)  73 us
    all_to_all x1, blocking collectives, exchange(): return lax.all_to_all(value, axis, 0, 0, axis_index_groups=groups)  45.4 us
    all_gather x1, waiting for transfers between devices, shards(): lax.all_gather(seed_grad.astype(jnp.bfloat16), 'fsdp', axis=0, tiled=True)  40.5 us
    pallas_call x1, Pallas kernels, orthonormal(): pl.pallas_call(orthonormal_kernel, out_shape=jax.ShapeDtypeStruct(matrix....  38.5 us
    all_to_all x6, starting transfers between devices, exchange(): return lax.all_to_all(value, axis, 0, 0, axis_index_groups=groups)  31.8 us
    all_gather x1, waiting for transfers between devices, shards(): fed = lax.all_gather(normed_two, 'fsdp', axis=0, tiled=True)  30.4 us
    all_gather x1, waiting for transfers between devices, shards(): whole_out = lax.all_gather(w_out, 'fsdp', axis=0, tiled=True)  28.7 us
  transfers between devices with their start and end apart: 24, of which 20 were waited for; matrix products, arithmetic and copies ran while one was open for 17% of the time, Pallas kernels for 5%

profile of v1, /device:TPU:1, one launch (start us, length us, event | category | flops | bytes accessed | tf_op | source)
XLA Modules:
  0.0 752.7 jit_solution(11673985772016526202)
XLA Ops:
  12.2 73.0 %all-gather.6.cloned.1.call-done = bf16[1024,3072]{1,0:T(8,128)(2,1)} async-done(((bf16[128,3072]{1,0:T(8,128)(2,1)}), bf16[1024,3072]{1,0:T(8,128)(2,1)}) %all-gather.6.cloned.1.call-update) | async-done | bytes 6291472 | tf_op jit(solution)/shard_map/all_gather | solution.py:230
  85.2 4.6 fusion.69
  93.6 28.7 %all-gather.8.cloned.1.call-done = bf16[1024,1024]{1,0:T(8,128)(2,1)} async-done(((bf16[128,1024]{1,0:T(8,128)(2,1)}), bf16[1024,1024]{1,0:T(8,128)(2,1)}) %all-gather.8.cloned.1.call-update) | async-done | bytes 2097168 | tf_op jit(solution)/shard_map/all_gather | solution.py:231
  122.3 2.4 multiply_reduce_fusion.6
  125.8 2.2 fusion.41
  129.5 4.4 all-to-all-start
  135.4 19.7 %all-to-all-done = bf16[8,128,576]{1,2,0:T(8,128)(2,1)} async-done(((bf16[8,128,576]{1,2,0:T(8,128)(2,1)}), bf16[8,128,576]{1,2,0:T(8,128)(2,1)}, u32[]{:S(2)}, u32[]{:S(2)}) %all-to-all-start) | async-done | bytes 1179680 | tf_op jit(solution)/shard_map/all_to_all | solution.py:66
  155.1 4.2 all-to-all-start.1
  160.7 19.8 %all-to-all-done.1 = bf16[8,128,576]{1,2,0:T(8,128)(2,1)} async-done(((bf16[8,128,576]{1,2,0:T(8,128)(2,1)}), bf16[8,128,576]{1,2,0:T(8,128)(2,1)}, u32[]{:S(2)}, u32[]{:S(2)}) %all-to-all-start.1) | async-done | bytes 1179680 | tf_op jit(solution)/shard_map/all_to_all | solution.py:66
  180.5 8.6 %all-to-all-start.2 = ((bf16[8,128,576]{1,2,0:T(8,128)(2,1)}), bf16[8,128,576]{1,2,0:T(8,128)(2,1)S(1)}, u32[]{:S(2)}, u32[]{:S(2)}) async-start(bf16[8,128,576]{1,2,0:T(8,128)(2,1)} %bitcast.14), calls=%async_computation.2 | async-start | bytes 2359296 | tf_op jit(solution)/shard_map/all_to_all | solution.py:66
  189.4 30.4 %all-gather.10.cloned.1.call-done = bf16[2048,1024]{1,0:T(8,128)(2,1)} async-done(((bf16[256,1024]{1,0:T(8,128)(2,1)}), bf16[2048,1024]{1,0:T(8,128)(2,1)}) %all-gather.10.cloned.1.call-update) | async-done | bytes 4194320 | tf_op jit(solution)/shard_map/all_gather | solution.py:257
  219.8 7.5 fusion.22
  227.3 5.6 fusion.18
  232.9 40.5 %all-gather.12.cloned.1.call-done = bf16[2048,1024]{1,0:T(8,128)(2,1)} async-done(((bf16[256,1024]{1,0:T(8,128)(2,1)}), bf16[2048,1024]{1,0:T(8,128)(2,1)}) %all-gather.12.cloned.1.call-update) | async-done | bytes 4194320 | tf_op jit(solution)/shard_map/all_gather | solution.py:235
  273.4 9.6 %multiply_convert_fusion = (bf16[2048,576]{0,1:T(8,128)(2,1)}, bf16[2048,576]{0,1:T(8,128)(2,1)}, bf16[2048,576]{0,1:T(8,128)(2,1)S(1)}) fusion(f32[2048,576]{0,1:T(8,128)} %fusion.22, f32[2048,576]{0,1:T(8,128)} %fusion.18, bf16[2048,1024]{1,0:T(8,128)(2,1)} %all-gather.12.cloned.1.call-done, bf16[8,128,576]{1,2,0:T(8,128)(2,1)S(1)} %all-to-all-done.2), kind=kOutput, calls=%fused_computation.10 | convolution fusion | flops 2434793472 | bytes 21889024 | tf_op jit(solution)/shard_map/dot_general | solution.py:262
  284.4 5.1 convolution_convert_fusion
  289.6 5.6 fusion.20
  295.2 6.6 add_convert_fusion
  301.8 5.0 all-to-all-start.3
  306.8 7.0 fusion.72
  313.8 66.4 %all-to-all-done.3 = bf16[8,256,1024]{2,1,0:T(8,128)(2,1)} async-done(((bf16[8,256,1024]{2,1,0:T(8,128)(2,1)}), bf16[8,256,1024]{2,1,0:T(8,128)(2,1)}, u32[]{:S(2)}, u32[]{:S(2)}) %all-to-all-start.3) | async-done | bytes 4194336 | tf_op jit(solution)/shard_map/all_to_all | solution.py:66
  380.2 3.2 convert_reduce_fusion
  385.2 17.8 %reduce-scatter.2.cloned.1.call-done = bf16[256,1024]{1,0:T(8,128)(2,1)} async-done(((bf16[2048,1024]{1,0:T(8,128)(2,1)}), bf16[256,1024]{1,0:T(8,128)(2,1)}) %reduce-scatter.2.cloned.1.call-update) | async-done | bytes 524304 | tf_op jit(solution)/shard_map/reduce_scatter | solution.py:268
  403.0 3.2 subtract_add_fusion.1
  406.2 3.1 multiply_reduce_fusion
  411.4 2.4 collective-permute-done.1
  415.4 6.4 fusion.51
  421.8 5.7 pad_maximum_fusion
  427.5 3.0 fusion.1
  430.5 2.7 collective-permute-start.9
  433.2 8.1 %fusion.71 = f32[1024,576]{0,1:T(8,128)S(1)} fusion(bf16[2048,576]{0,1:T(8,128)(2,1)} %get-tuple-element.116, bf16[2048,1024]{1,0:T(8,128)(2,1)} %all-gather.10.cloned.1.call-done), kind=kOutput, calls=%fused_computation.161 | convolution fusion | flops 2415919104 | bytes 8912896 | tf_op jit(solution)/shard_map/dot_general | solution.py:58
  441.4 2.7 fusion.70
  444.0 3.3 pad_maximum_fusion.1
  447.4 8.1 %copy.161 = f32[1024,1728]{1,0:T(8,128)} copy(f32[1024,1728]{0,1:T(8,128)} %pad_maximum_fusion.1) | data formatting | bytes 14155776 | tf_op jit(solution)/shard_map/concatenate | solution.py:271
  455.5 3.6 fusion.3
  460.2 3.8 collective-permute-done.10
  463.9 4.3 fusion.2
  468.2 5.0 all-to-all-start.5
  473.2 8.0 %fusion = bf16[8,64,4096]{2,1,0:T(8,128)(2,1)} fusion(bf16[8,64,4096]{2,1,0:T(8,128)(2,1)} %collective-permute-done.9, f32[8,2,64,4096]{3,2,1,0:T(8,128)} %bitcast.229, s32[]{:T(128)S(6)} %select_n.99), kind=kLoop, calls=%fused_computation.4 | loop fusion | flops 6291456 | bytes 16777220 | tf_op jit(solution)/shard_map/convert_element_type | solution.py:301
  481.3 16.3 %all-to-all-done.5 = bf16[8,64,1728]{2,1,0:T(8,128)(2,1)} async-done(((bf16[8,64,1728]{2,1,0:T(8,128)(2,1)}), bf16[8,64,1728]{2,1,0:T(8,128)(2,1)}, u32[]{:S(2)}, u32[]{:S(2)}) %all-to-all-start.5) | async-done | bytes 1769504 | tf_op jit(solution)/shard_map/all_to_all | solution.py:66
  497.6 4.6 all-to-all-start.4
  502.9 6.3 reshape.300
  509.2 5.3 copy.162
  514.4 4.1 reshape.301
  518.6 33.2 %all-to-all-done.4 = bf16[8,64,4096]{2,1,0:T(8,128)(2,1)} async-done(((bf16[8,64,4096]{2,1,0:T(8,128)(2,1)}), bf16[8,64,4096]{2,1,0:T(8,128)(2,1)}, u32[]{:S(2)}, u32[]{:S(2)}) %all-to-all-start.4) | async-done | bytes 4194336 | tf_op jit(solution)/shard_map/all_to_all | solution.py:66
  551.8 2.9 reduce_sum.151
  554.7 3.5 bitcast_bitcast_fusion
  558.2 4.3 gather_fusion
  562.6 2.2 select_select_fusion
  564.8 45.4 %all_to_all.35 = bf16[8,24,64,128]{3,2,1,0:T(8,128)(2,1)S(1)} all-to-all(bf16[8,24,64,128]{3,2,1,0:T(8,128)(2,1)S(1)} %select_select_fusion), channel_id=1, replica_groups={{0,16,32,48,64,80,96,112},{8,24,40,56,72,88,104,120},{1,17,33,49,65,81,..., dimensions={0} | all-to-all | bytes 6291456 | tf_op jit(solution)/shard_map/all_to_all | solution.py:66
  610.8 2.5 collective-permute-start.11
  621.1 2.8 fusion.68
  625.5 6.2 multiply_reduce_fusion.4
  633.1 6.8 collective-permute-start.3
  641.5 4.4 collective-permute-start.4
  647.8 2.6 collective-permute-done.5
  654.8 2.9 collective-permute-done.7
  659.6 2.5 collective-permute-done.8
  670.1 38.5 %shard_map.280 = f32[24,128,128]{2,1,0:T(8,128)} custom-call(f32[24,128,128]{2,1,0:T(8,128)S(1)} %bitcast.227), custom_call_target="tpu_custom_call" | custom-call | tf_op jit(solution)/shard_map/pallas_call | solution.py:168
  709.6 10.4 %gather_fusion.1 = bf16[140,128,128]{2,1,0:T(8,128)(2,1)} fusion(bf16[192,128,128]{2,1,0:T(8,128)(2,1)} %all-gather.14.cloned.1.call-done, s32[1024]{0:T(1024)S(1)} %pad_clamp_fusion), kind=kCustom, calls=%fused_computation.1 | custom fusion | bytes 9175600 | tf_op jit(solution)/shard_map/jit(_take)/gather | solution.py:351
  720.0 5.0 select_bitcast_fusion
  724.9 6.6 copy.171
  735.2 2.2 fusion.66
  737.4 2.3 copy.178
  (181 shorter events, 62.5 us)
Async XLA Ops:
  7.2 78.0 %all-gather.6.cloned.1.call-start = ((), (), s32[]{:S(2)}) async-start(), calls=%async_computation.8 | async-start | bytes 7077888 | tf_op jit(solution)/shard_map/all_gather | solution.py:230
  7.9 114.4 %all-gather.8.cloned.1.call-start = ((), (), s32[]{:S(2)}) async-start(), calls=%async_computation.9 | async-start | bytes 2359296 | tf_op jit(solution)/shard_map/all_gather | solution.py:231
  8.7 211.1 %all-gather.10.cloned.1.call-start = ((), (), s32[]{:S(2)}) async-start(), calls=%async_computation.10 | async-start | bytes 4718592 | tf_op jit(solution)/shard_map/all_gather | solution.py:257
  9.9 75.2 %copy-start.35 = (f32[256]{0:T(256)}, f32[256]{0:T(256)S(1)}, u32[]{:S(2)}) copy-start(f32[256]{0:T(256)S(1)} %rsqrt_bitcast_fusion) | copy-start | bytes 3076
  10.9 74.3 %copy-start.28 = (f32[1,1024]{1,0:T(1,128)}, f32[1,1024]{1,0:T(1,128)S(1)}, u32[]{:S(2)}) copy-start(f32[1,1024]{1,0:T(1,128)S(1)} %get-tuple-element.135) | copy-start | bytes 12292
  12.2 73.0 %copy-start.15 = (bf16[256,1024]{1,0:T(8,128)(2,1)}, bf16[256,1024]{1,0:T(8,128)(2,1)S(1)}, u32[]{:S(2)}) copy-start(bf16[256,1024]{1,0:T(8,128)(2,1)S(1)} %multiply_convert_fusion.4) | copy-start | bytes 1572868
  89.8 2.7 copy-start.1
  89.9 2.1 collective-permute-start
  92.1 30.2 %copy-start.7 = (bf16[2,1,128,1024]{3,2,1,0:T(8,128)(2,1)S(1)}, bf16[2,1,128,1024]{3,2,1,0:T(8,128)(2,1)}, u32[]{:S(2)}) copy-start(bf16[2,1,128,1024]{3,2,1,0:T(8,128)(2,1)} %param.17) | copy-start | bytes 1572868
  93.6 32.1 %copy-start.10 = (bf16[256,1024]{1,0:T(8,128)(2,1)}, bf16[256,1024]{1,0:T(8,128)(2,1)S(1)}, u32[]{:S(2)}) copy-start(bf16[256,1024]{1,0:T(8,128)(2,1)S(1)} %fusion.32) | copy-start | bytes 1572868
  122.3 3.5 copy-start.37
  125.7 2.5 copy-start.20
  125.7 147.7 %all-gather.12.cloned.1.call-start = ((), (), s32[]{:S(2)}) async-start(), calls=%async_computation.12 | async-start | bytes 4718592 | tf_op jit(solution)/shard_map/all_gather | solution.py:235
  129.5 4.4 copy-start.21
  129.5 25.5 %all-to-all-start = ((bf16[8,128,576]{1,2,0:T(8,128)(2,1)}), bf16[8,128,576]{1,2,0:T(8,128)(2,1)}, u32[]{:S(2)}, u32[]{:S(2)}) async-start(bf16[8,128,576]{1,2,0:T(8,128)(2,1)} %bitcast.10), calls=%async_computation | async-start | bytes 2359296 | tf_op jit(solution)/shard_map/all_to_all | solution.py:66
  135.4 23.9 %copy-start.22 = (bf16[128,4608]{1,0:T(8,128)(2,1)S(1)}, bf16[128,4608]{1,0:T(8,128)(2,1)}, u32[]{:S(2)}) copy-start(bf16[128,4608]{1,0:T(8,128)(2,1)} %param.27) | copy-start | bytes 3538948
  155.1 25.5 %all-to-all-start.1 = ((bf16[8,128,576]{1,2,0:T(8,128)(2,1)}), bf16[8,128,576]{1,2,0:T(8,128)(2,1)}, u32[]{:S(2)}, u32[]{:S(2)}) async-start(bf16[8,128,576]{1,2,0:T(8,128)(2,1)} %bitcast.12), calls=%async_computation.1 | async-start | bytes 2359296 | tf_op jit(solution)/shard_map/all_to_all | solution.py:66
  180.5 52.3 %all-to-all-start.2 = ((bf16[8,128,576]{1,2,0:T(8,128)(2,1)}), bf16[8,128,576]{1,2,0:T(8,128)(2,1)S(1)}, u32[]{:S(2)}, u32[]{:S(2)}) async-start(bf16[8,128,576]{1,2,0:T(8,128)(2,1)} %bitcast.14), calls=%async_computation.2 | async-start | bytes 2359296 | tf_op jit(solution)/shard_map/all_to_all | solution.py:66
  189.1 213.9 %reduce-scatter.2.cloned.1.call-start = ((), (), s32[]{:S(2)}) async-start(), calls=%async_computation.11 | async-start | bytes 4718592 | tf_op jit(solution)/shard_map/reduce_scatter | solution.py:268
  219.8 7.5 copy-start.38
  283.0 1.4 copy-start.42
  289.6 5.7 copy-start.41
  301.8 78.4 %all-to-all-start.3 = ((bf16[8,256,1024]{2,1,0:T(8,128)(2,1)}), bf16[8,256,1024]{2,1,0:T(8,128)(2,1)}, u32[]{:S(2)}, u32[]{:S(2)}) async-start(bf16[8,256,1024]{2,1,0:T(8,128)(2,1)} %bitcast.256), calls=%async_computation.4 | async-start | bytes 8388608 | tf_op jit(solution)/shard_map/all_to_all | solution.py:66
  403.0 3.2 copy-start.2
  403.0 3.2 copy-start.6
  406.2 4.4 copy-start.11
  409.3 4.5 copy-start.3
  409.3 5.2 copy-start.17
  409.4 4.5 collective-permute-start.1
  414.2 1.2 copy-start.16
  414.6 7.2 copy-start.18
  427.5 13.9 %copy-start = (f32[1024,4096]{1,0:T(8,128)}, f32[1024,4096]{1,0:T(8,128)S(1)}, u32[]{:S(2)}) copy-start(f32[1024,4096]{1,0:T(8,128)S(1)} %pad_maximum_fusion) | copy-start | bytes 50331652
  430.5 10.9 %copy-start.39 = (bf16[2048,1024]{1,0:T(8,128)(2,1)S(1)}, bf16[2048,1024]{1,0:T(8,128)(2,1)}, u32[]{:S(2)}) copy-start(bf16[2048,1024]{1,0:T(8,128)(2,1)} %all-gather.10.cloned.1.call-done) | copy-start | bytes 12582916
  430.5 10.9 %copy-start.40 = (bf16[2048,576]{0,1:T(8,128)(2,1)S(1)}, bf16[2048,576]{0,1:T(8,128)(2,1)}, u32[]{:S(2)}) copy-start(bf16[2048,576]{0,1:T(8,128)(2,1)} %get-tuple-element.117) | copy-start | bytes 7077892
  430.5 42.8 %collective-permute-start.9 = (bf16[8,64,4096]{2,1,0:T(8,128)(2,1)}, bf16[8,64,4096]{2,1,0:T(8,128)(2,1)}, u32[]{:S(2)}, u32[]{:S(2)}) collective-permute-start(bf16[8,64,4096]{2,1,0:T(8,128)(2,1)} %fusion.1), channel_id=1, source_target_pairs={{0,8},{8,0},{16,24},{24,16},{32,40},{40,32},{48,56},{56,48},{64,72... | collective-permute-start | bytes 12582920 | tf_op jit(solution)/shard_map/ppermute | solution.py:36
  441.4 2.7 copy-start.14
  459.1 4.9 collective-permute-start.10
  468.2 29.4 %all-to-all-start.5 = ((bf16[8,64,1728]{2,1,0:T(8,128)(2,1)}), bf16[8,64,1728]{2,1,0:T(8,128)(2,1)}, u32[]{:S(2)}, u32[]{:S(2)}) async-start(bf16[8,64,1728]{2,1,0:T(8,128)(2,1)} %fusion.2), calls=%async_computation.6 | async-start | bytes 3670016 | tf_op jit(solution)/shard_map/all_to_all | solution.py:66
  481.3 21.0 %copy-start.32 = (s32[1,140]{1,0:T(1,128)S(1)}, s32[1,140]{1,0:T(1,128)}, u32[]{:S(2)}) copy-start(s32[1,140]{1,0:T(1,128)} %param.28) | copy-start | bytes 1684
  497.6 54.1 %all-to-all-start.4 = ((bf16[8,64,4096]{2,1,0:T(8,128)(2,1)}), bf16[8,64,4096]{2,1,0:T(8,128)(2,1)}, u32[]{:S(2)}, u32[]{:S(2)}) async-start(bf16[8,64,4096]{2,1,0:T(8,128)(2,1)} %fusion), calls=%async_computation.5 | async-start | bytes 8388608 | tf_op jit(solution)/shard_map/all_to_all | solution.py:66
  502.2 207.4 %all-gather.14.cloned.1.call-start = ((), (), s32[]{:S(2)}) async-start(), calls=%async_computation.13 | async-start | bytes 6684672 | tf_op jit(solution)/shard_map/all_gather | solution.py:350
  610.8 4.1 collective-permute-start.11
  613.3 3.1 copy-start.25
  614.9 2.5 copy-start.12
  617.5 2.7 copy-start.26
  619.0 2.1 copy-start.24
  621.1 4.4 copy-start.29
  621.1 4.4 copy-start.36
  625.5 6.3 copy-start.33
  625.5 6.2 copy-start.34
  631.7 26.5 %copy-start.8 = (bf16[2,1,128,1024]{3,2,1,0:T(8,128)(2,1)S(1)}, bf16[2,1,128,1024]{3,2,1,0:T(8,128)(2,1)}, u32[]{:S(2)}) copy-start(bf16[2,1,128,1024]{3,2,1,0:T(8,128)(2,1)} %param.17) | copy-start | bytes 1572868
  631.8 26.5 %copy-start.23 = (f32[256,1024]{1,0:T(8,128)S(1)}, f32[256,1024]{1,0:T(8,128)}, u32[]{:S(2)}) copy-start(f32[256,1024]{1,0:T(8,128)} %get-tuple-element.138) | copy-start | bytes 3145732
  631.8 1.3 collective-permute-start.2
  633.1 8.4 %collective-permute-start.3 = (f32[5,1024]{1,0:T(8,128)S(1)}, f32[5,1024]{1,0:T(8,128)S(1)}, u32[]{:S(2)}, u32[]{:S(2)}) collective-permute-start(f32[5,1024]{1,0:T(8,128)S(1)} %add.221), channel_id=1, source_target_pairs={{0,1},{1,0},{2,3},{3,2},{4,5},{5,4},{6,7},{7,6},{8,9},{9,8},{10,11... | collective-permute-start | bytes 61448 | tf_op jit(solution)/shard_map/ppermute | solution.py:36
  641.5 5.7 collective-permute-start.4
  647.2 3.2 collective-permute-start.5
  650.4 3.0 collective-permute-start.6
  652.9 9.2 %copy-start.27 = (f32[5,1024]{1,0:T(8,128)S(1)}, f32[5,1024]{1,0:T(8,128)}, u32[]{:S(2)}) copy-start(f32[5,1024]{1,0:T(8,128)} %param.20) | copy-start | bytes 61444
  652.9 9.2 %copy-start.30 = (f32[5,1024]{1,0:T(8,128)S(1)}, f32[5,1024]{1,0:T(8,128)}, u32[]{:S(2)}) copy-start(f32[5,1024]{1,0:T(8,128)} %param.21) | copy-start | bytes 61444
  652.9 9.2 %copy-start.31 = (f32[5,1024]{1,0:T(8,128)S(1)}, f32[5,1024]{1,0:T(8,128)}, u32[]{:S(2)}) copy-start(f32[5,1024]{1,0:T(8,128)} %param.22) | copy-start | bytes 61444
  653.4 4.3 collective-permute-start.7
  657.7 4.4 collective-permute-start.8
  666.4 2.0 copy-start.9
  670.1 38.5 %copy-start.13 = (f32[1,12,128,128]{3,2,1,0:T(8,128)S(1)}, f32[1,12,128,128]{3,2,1,0:T(8,128)}, u32[]{:S(2)}) copy-start(f32[1,12,128,128]{3,2,1,0:T(8,128)} %param.30) | copy-start | bytes 2359300
  (3 other events, 2.7 us)
Sparse Core Ops, SparseCore 0:
  9.7 75.4 all-gather.5
  86.8 35.3 all-gather.7
  125.8 93.9 all-gather.9
  221.9 51.5 all-gather.11
  289.7 113.3 reduce-scatter.1
  624.0 69.0 all-gather.13
